TPU v7x, 32 devices: a whole 2x2x4 slice. The times are simulated.
32 devices in a mesh: groups: 2 (over x), wide: 16 (over z, y, core).
Axes of the slice: x: 2, y: 2, z: 4, core: 2. Of those that a mesh axis runs over, the one named last changes fastest.
Arguments:
- tokens: bfloat16 [2, 64, 18432], P(None, 'groups', 'wide'), parts along dimension 1, may hold values from -360 to 360
- norm_gain: float32 [18432], replicated, may hold values from 0.1 to 1.9
- w_qkv: bfloat16 [18432, 12800], P(None, 'wide'), may hold values from -0.046875 to 0.046875
- w_out: bfloat16 [12288, 18432], P(None, 'wide'), may hold values from -0.0546875 to 0.0546875
- cache_k: bfloat16 [64, 2048, 256], P(('groups', 'wide')), parts along dimension 0, may hold values from -6 to 6
- cache_v: bfloat16 [64, 2048, 256], P(('groups', 'wide')), parts along dimension 0, may hold values from -6 to 6
- lengths: int32 [64], P(('groups', 'wide')), parts along dimension 0, may hold values from 1 to 2048, as said below
Outputs:
- attended: bfloat16 [2, 64, 18432], P(None, 'groups', 'wide'), parts along dimension 1
There are 2 independent parts, one for each index of `groups`. A program takes and returns all parts, laid end to end along the dimension named above; an argument that names none is the same for every part. Nothing has to cross between parts.
Inputs may be any that keep to these rules, and one draw needn't show every extreme that they name: Sequence b uses cache slots 0 to lengths[b] - 1; some sequence has 2048.
All inputs are finite; a program needn't handle non-finite values.
Results may differ from a plain program's by a relative error of at most 0.01.
Values may be sent and summed in bfloat16 or wider, within the bound.
A program may use at most 128 MiB of HBM per device.

v0:
```python
import math

import jax
import jax.numpy as jnp
from jax import lax
from jax.sharding import PartitionSpec as P

norm_eps = 1e-05


def rotate(values, cosine, sine_table):
    half = values.shape[-1] // 2
    first = values[..., :half]
    second = values[..., half:]
    return jnp.concatenate(
        [first * cosine - second * sine_table, second * cosine + first * sine_table], axis=-1
    )


def attend(projected, cache_k, cache_v, lengths, heads, head_dim):
    step_count, seq_rows, _ = projected.shape
    width_q = heads * head_dim
    query = (
        projected[..., :width_q].astype(jnp.float32).reshape(step_count, seq_rows, heads, head_dim)
    )
    key_new = projected[..., width_q : width_q + head_dim].astype(jnp.float32)
    value_new = projected[..., width_q + head_dim :]
    positions = lengths[None, :] + jnp.arange(step_count, dtype=jnp.int32)[:, None]
    half = head_dim // 2
    freqs = jnp.exp(jnp.arange(half, dtype=jnp.float32) * (-2.0 * math.log(10000.0) / head_dim))
    angles = positions.astype(jnp.float32)[..., None] * freqs
    cosine = jnp.cos(angles)
    sine_table = jnp.sin(angles)
    query = rotate(query, cosine[:, :, None, :], sine_table[:, :, None, :]).astype(jnp.bfloat16)
    key_new = rotate(key_new, cosine, sine_table).astype(jnp.bfloat16)
    scale = 1.0 / math.sqrt(head_dim)
    cache_scores = (
        jnp.einsum("snhd,nld->snhl", query, cache_k, preferred_element_type=jnp.float32) * scale
    )
    slots = jnp.arange(cache_k.shape[1], dtype=jnp.int32)
    valid = slots[None, :] < lengths[:, None]
    cache_scores = jnp.where(valid[None, :, None, :], cache_scores, -1e30)
    new_scores = (
        jnp.einsum("snhd,tnd->snht", query, key_new, preferred_element_type=jnp.float32) * scale
    )
    order = jnp.arange(step_count, dtype=jnp.int32)
    causal = order[None, :] <= order[:, None]
    new_scores = jnp.where(causal[:, None, None, :], new_scores, -1e30)
    top = jnp.maximum(jnp.max(cache_scores, axis=-1), jnp.max(new_scores, axis=-1))
    exp_cache = jnp.exp(cache_scores - top[..., None])
    exp_new = jnp.exp(new_scores - top[..., None])
    denom = jnp.sum(exp_cache, axis=-1) + jnp.sum(exp_new, axis=-1)
    w_cache = (exp_cache / denom[..., None]).astype(jnp.bfloat16)
    w_new = (exp_new / denom[..., None]).astype(jnp.bfloat16)
    mixed = jnp.einsum("snhl,nld->snhd", w_cache, cache_v, preferred_element_type=jnp.float32)
    mixed = mixed + jnp.einsum(
        "snht,tnd->snhd", w_new, value_new, preferred_element_type=jnp.float32
    )
    return mixed.reshape(step_count, seq_rows, width_q).astype(jnp.bfloat16)


def on_device(tokens, norm_gain, w_qkv, w_out, cache_k, cache_v, lengths):
    gathered = lax.all_gather(tokens, "wide", axis=2, tiled=True)
    widened = gathered.astype(jnp.float32)
    center = jnp.mean(widened, axis=-1, keepdims=True)
    spread = jnp.mean(widened * widened, axis=-1, keepdims=True) - center * center
    normed = ((widened - center) * lax.rsqrt(spread + norm_eps) * norm_gain).astype(jnp.bfloat16)
    projected = jnp.einsum("sbd,dc->sbc", normed, w_qkv, preferred_element_type=jnp.float32)
    projected = projected.astype(jnp.bfloat16)
    per_sequence = lax.all_to_all(projected, "wide", split_axis=1, concat_axis=2, tiled=True)
    head_dim = cache_k.shape[2]
    heads = per_sequence.shape[2] // head_dim - 2
    mixed = attend(per_sequence, cache_k, cache_v, lengths, heads, head_dim)
    result = jnp.einsum(
        "snh,hd->snd",
        lax.all_gather(mixed, "wide", axis=1, tiled=True),
        w_out,
        preferred_element_type=jnp.float32,
    )
    return result.astype(jnp.bfloat16)


def solution(mesh):
    placed = (
        P(None, "groups", "wide"),
        P(),
        P(None, "wide"),
        P(None, "wide"),
        P(("groups", "wide"), None, None),
        P(("groups", "wide"), None, None),
        P(("groups", "wide")),
    )
    return jax.shard_map(
        on_device, mesh=mesh, in_specs=placed, out_specs=P(None, "groups", "wide"), check_vma=False
    )
```

profile of v0, /device:TPU:0, one launch (start us, length us, event | category | flops | bytes accessed | tf_op | source)
XLA Modules:
  0.0 146.9 jit_solution(9520849248416865843)
XLA Ops:
  6.5 0.0 copy-start
  6.5 0.0 copy-start.3
  6.5 0.0 all-gather.3.cloned.1.call-start
  6.5 0.7 all-gather.3.cloned.1.call-update
  7.3 0.7 iota_compare_fusion
  8.0 46.7 %all-gather.3.cloned.1.call-done = bf16[2,32,18432]{2,1,0:T(8,128)(2,1)} async-done(((bf16[2,32,1152]{2,1,0:T(8,128)(2,1)}), bf16[2,32,18432]{2,1,0:T(8,128)(2,1)}) %all-gather.3.cloned.1.call-update) | async-done | bytes 2359312 | tf_op jit(solution)/shard_map/all_gather | solution.py:63
  54.8 0.0 copy-start.2
  54.8 2.6 %convert_reduce_fusion = (f32[2,32]{1,0:T(2,128)S(1)}, f32[2,32]{1,0:T(2,128)S(1)}) fusion(bf16[2,32,18432]{2,1,0:T(8,128)(2,1)} %all-gather.3.cloned.1.call-done), kind=kLoop, calls=%fused_computation.6 | loop fusion | flops 4718464 | bytes 2359808 | tf_op jit(solution)/shard_map/reduce_sum | solution.py:65
  57.4 0.0 copy-done.3
  57.4 0.0 copy-done.2
  57.4 0.0 copy-start.4
  57.4 13.9 %fusion.28 = bf16[2,32,800]{2,1,0:T(8,128)(2,1)S(1)} fusion(bf16[18432,800]{0,1:T(8,128)(2,1)} %param.9, bf16[2,32,18432]{2,1,0:T(8,128)(2,1)S(1)} %copy-done.2, f32[18432]{0:T(1024)S(1)} %copy-done.3, f32[2,32]{1,0:T(2,128)S(1)} %get-tuple-element.14, f32[2,32]{1,0:T(2,128)S(1)} %get-tuple-element.13), kind=kOutput, calls=%fused_computation.28 | convolution fusion | flops 1893386240 | bytes 32027136 | tf_op jit(solution)/shard_map/sbd,dc->sbc/dot_general | solution.py:68
  71.4 0.7 copy.10
  72.1 3.5 %all-to-all-start = ((bf16[2,32,800]{2,0,1:T(2,128)(2,1)}), bf16[2,32,800]{2,0,1:T(2,128)(2,1)S(1)}, u32[]{:S(2)}, u32[]{:S(2)}) async-start(bf16[2,32,800]{2,0,1:T(2,128)(2,1)} %copy.10), calls=%async_computation | async-start | bytes 229376 | tf_op jit(solution)/shard_map/all_to_all | solution.py:70
  75.6 0.0 all-gather.5.cloned.1.call-start
  75.7 0.0 copy-done.4
  75.7 0.1 add_convert_fusion.2
  75.8 7.5 %all-to-all-done = bf16[2,32,800]{2,0,1:T(2,128)(2,1)S(1)} async-done(((bf16[2,32,800]{2,0,1:T(2,128)(2,1)}), bf16[2,32,800]{2,0,1:T(2,128)(2,1)S(1)}, u32[]{:S(2)}, u32[]{:S(2)}) %all-to-all-start) | async-done | bytes 102432 | tf_op jit(solution)/shard_map/all_to_all | solution.py:70
  83.3 0.2 all_to_all.16
  83.5 0.1 slice_convert_fusion
  83.6 0.2 reshape.96
  83.8 0.1 subtract_convert_fusion.1
  84.0 0.0 copy-done
  84.0 0.0 copy-start.5
  84.0 0.8 fusion.47
  84.8 0.2 fusion.48
  85.0 0.4 fusion.21
  85.4 0.2 convolution_bitcast_fusion
  85.7 0.0 copy-done.5
  85.7 0.5 fusion.33
  86.2 0.7 convert_element_type.45
  86.9 0.0 all-gather.5.cloned.1.call-update
  86.9 37.4 %all-gather.5.cloned.1.call-done = bf16[2,32,12288]{2,0,1:T(2,128)(2,1)} async-done(((bf16[2,2,12288]{2,0,1:T(2,128)(2,1)}), bf16[2,32,12288]{2,0,1:T(2,128)(2,1)}) %all-gather.5.cloned.1.call-update) | async-done | bytes 1572880 | tf_op jit(solution)/shard_map/all_gather | solution.py:76
  124.3 0.0 copy-start.1
  124.3 15.8 %fusion.14 = bf16[2,32,1152]{2,1,0:T(8,128)(2,1)} fusion(bf16[12288,1152]{1,0:T(8,128)(2,1)} %param.10, bf16[2,32,12288]{2,0,1:T(2,128)(2,1)} %all-gather.5.cloned.1.call-done), kind=kOutput, calls=%fused_computation.17 | convolution fusion | flops 1812013056 | bytes 30031872 | tf_op jit(solution)/shard_map/snh,hd->snd/dot_general | solution.py:74
  140.1 0.0 copy-done.1
  (9 shorter events, 0.1 us)
Async XLA Ops:
  6.5 77.4 %copy-start = (bf16[2,2048,256]{2,1,0:T(8,128)(2,1)S(1)}, bf16[2,2048,256]{2,1,0:T(8,128)(2,1)}, u32[]{:S(2)}) copy-start(bf16[2,2048,256]{2,1,0:T(8,128)(2,1)} %param.11) | copy-start | bytes 6291460
  6.5 50.9 %copy-start.3 = (f32[18432]{0:T(1024)S(1)}, f32[18432]{0:T(1024)}, u32[]{:S(2)}) copy-start(f32[18432]{0:T(1024)} %param.8) | copy-start | bytes 221188
  6.5 48.2 %all-gather.3.cloned.1.call-start = ((), (), s32[]{:S(2)}) async-start(), calls=%async_computation.1 | async-start | bytes 2506752 | tf_op jit(solution)/shard_map/all_gather | solution.py:63
  54.8 2.6 %copy-start.2 = (bf16[2,32,18432]{2,1,0:T(8,128)(2,1)S(1)}, bf16[2,32,18432]{2,1,0:T(8,128)(2,1)}, u32[]{:S(2)}) copy-start(bf16[2,32,18432]{2,1,0:T(8,128)(2,1)} %all-gather.3.cloned.1.call-done) | copy-start | bytes 7077892
  57.4 18.3 %copy-start.4 = (s32[2]{0:T(128)S(1)}, s32[2]{0:T(128)}, u32[]{:S(2)}) copy-start(s32[2]{0:T(128)} %param.13) | copy-start | bytes 28
  72.1 11.2 %all-to-all-start = ((bf16[2,32,800]{2,0,1:T(2,128)(2,1)}), bf16[2,32,800]{2,0,1:T(2,128)(2,1)S(1)}, u32[]{:S(2)}, u32[]{:S(2)}) async-start(bf16[2,32,800]{2,0,1:T(2,128)(2,1)} %copy.10), calls=%async_computation | async-start | bytes 229376 | tf_op jit(solution)/shard_map/all_to_all | solution.py:70
  75.6 48.7 %all-gather.5.cloned.1.call-start = ((), (), s32[]{:S(2)}) async-start(), calls=%async_computation.2 | async-start | bytes 1671168 | tf_op jit(solution)/shard_map/all_gather | solution.py:76
  84.0 1.7 %copy-start.5 = (bf16[2,2048,256]{2,1,0:T(8,128)(2,1)S(1)}, bf16[2,2048,256]{2,1,0:T(8,128)(2,1)}, u32[]{:S(2)}) copy-start(bf16[2,2048,256]{2,1,0:T(8,128)(2,1)} %param.12) | copy-start | bytes 6291460
  124.3 15.8 %copy-start.1 = (bf16[2,2048,256]{2,1,0:T(8,128)(2,1)S(1)}, bf16[2,2048,256]{2,1,0:T(8,128)(2,1)}, u32[]{:S(2)}) copy-start(bf16[2,2048,256]{2,1,0:T(8,128)(2,1)} %param.11) | copy-start | bytes 6291460
Sparse Core Ops, SparseCore 0:
  9.7 45.0 all-gather.2
  87.0 37.2 all-gather.4
where the time goes:
time: 147 us
  waiting for transfers between devices  92.4 us (63%)
  matrix products  31.5 us (21%)
  between operations  13.5 us (9%)
  other arithmetic  4.07 us (3%)
  starting transfers between devices  3.57 us (2%)
  local copies, waits for them, and re-layouts  1.81 us (1%)
    all_gather x1, waiting for transfers between devices, on_device(): gathered = lax.all_gather(tokens, 'wide', axis=2, tiled=True)  46.7 us
    all_gather x1, waiting for transfers between devices, on_device(): lax.all_gather(mixed, 'wide', axis=1, tiled=True)  37.4 us
    dot_general x1, matrix products, on_device(): jnp.einsum('snh,hd->snd', lax.all_gather(mixed, 'wide', axis=1, tiled=Tru...  15.8 us
    dot_general x1, matrix products, on_device(): jnp.einsum('sbd,dc->sbc', normed, w_qkv, preferred_element_type=jnp.float32)  13.9 us
    all_to_all x1, waiting for transfers between devices, on_device(): lax.all_to_all(projected, 'wide', split_axis=1, concat_axis=2, tiled=True)  7.54 us
    all_to_all x1, starting transfers between devices, on_device(): lax.all_to_all(projected, 'wide', split_axis=1, concat_axis=2, tiled=True)  3.53 us
  transfers between devices with their start and end apart: 3, of which 3 were waited for; matrix products, arithmetic and copies ran while one was open for 1% of the time, Pallas kernels for 0%

commit v1 on v0

--- a/solution.py
+++ b/solution.py
@@ -1,11 +1,20 @@
+import functools
 import math
 
 import jax
 import jax.numpy as jnp
 from jax import lax
+from jax.experimental import pallas as pl
+from jax.experimental.pallas import tpu as pltpu
 from jax.sharding import PartitionSpec as P
 
 norm_eps = 1e-05
+MESH = pl.DeviceIdType.MESH
+Z, Y, C = 4, 2, 2
+WIDE = Z * Y * C
+SLOTS = 8
+PIECES = 4
+GROUP = 4
 
 
 def rotate(values, cosine, sine_table):
@@ -80,6 +89,591 @@
     return result.astype(jnp.bfloat16)
 
 
+def iota(shape, axis):
+    return lax.broadcasted_iota(jnp.int32, shape, axis)
+
+
+def pick(mask):
+    return jnp.where(mask, 1.0, 0.0).astype(jnp.bfloat16)
+
+
+def dot(a, b):
+    return jnp.dot(a, b, preferred_element_type=jnp.float32)
+
+
+def dot_t(a, b):
+    return lax.dot_general(a, b, (((1,), (1,)), ((), ())), preferred_element_type=jnp.float32)
+
+
+def fused_kernel(
+    lengths,
+    tokens,
+    gain,
+    cos_ref,
+    sin_ref,
+    w_qkv,
+    w_out,
+    cache_k,
+    cache_v,
+    out,
+    shards,
+    stats,
+    w_in,
+    w_last,
+    keys,
+    values,
+    acc,
+    to_send,
+    arrived,
+    gathered,
+    total,
+    columns,
+    local_sem,
+    last_sem,
+    cache_sem,
+    stat_send,
+    stat_recv,
+    send_z,
+    send_y,
+    send_c,
+    recv1,
+    all_send,
+    all_recv,
+    send2_z,
+    send2_y,
+    send2_c,
+    recv2,
+):
+    me = lax.axis_index("wide")
+    z = me // (Y * C)
+    y = (me // C) % Y
+    c = me % C
+    depth = tokens.shape[1]
+    rows = tokens.shape[0]
+    seqs = rows // 2
+    out_depth = w_last.shape[1]
+    width = w_qkv.shape[1]
+    heads = w_out.shape[0] // 256
+    groups = heads // GROUP
+    mirrored = (z + z // 2) % 2
+    upper = z // 2
+
+    def z_at(p):
+        m = p + mirrored * (1 - 2 * p) * (1 - p // 2)
+        return m + upper * (3 - 2 * m)
+
+    def index(zz, yy, cc):
+        return (zz * Y + yy) * C + cc
+
+    def remote(src, dst, send_sem, recv_sem, target):
+        return pltpu.make_async_remote_copy(
+            src_ref=src,
+            dst_ref=dst,
+            send_sem=send_sem,
+            recv_sem=recv_sem,
+            device_id={"wide": target},
+            device_id_type=MESH,
+        )
+
+    y_peer = index(z, 1 - y, c)
+    c_peer = index(z, y, 1 - c)
+
+    def load_in(owner):
+        return pltpu.make_async_copy(
+            w_qkv.at[pl.ds(pl.multiple_of(owner * depth, depth), depth)],
+            w_in.at[owner],
+            local_sem.at[owner],
+        )
+
+    def load_last(g):
+        return pltpu.make_async_copy(
+            w_out.at[pl.ds(pl.multiple_of(g * out_depth, out_depth), out_depth)],
+            w_last.at[g % SLOTS],
+            last_sem.at[g],
+        )
+
+    load_keys = pltpu.make_async_copy(cache_k, keys, cache_sem.at[0])
+    load_values = pltpu.make_async_copy(cache_v, values, cache_sem.at[1])
+
+    def load_round(p, carry):
+        @pl.when(p <= 3)
+        def _():
+            load_in(index(z_at(p), y, c)).start()
+            load_in(index(z_at(p), y, 1 - c)).start()
+
+        @pl.when(p >= 1)
+        def _():
+            load_in(index(z_at(p - 1), 1 - y, c)).start()
+            load_in(index(z_at(p - 1), 1 - y, 1 - c)).start()
+
+        return carry
+
+    lax.fori_loop(0, 5, load_round, 0)
+
+    barrier = pltpu.get_barrier_semaphore()
+
+    def greet(k, carry):
+        pl.semaphore_signal(
+            barrier, inc=1, device_id={"wide": (me + k) % WIDE}, device_id_type=MESH
+        )
+        return carry
+
+    lax.fori_loop(1, WIDE, greet, 0)
+
+    widened = tokens[...].astype(jnp.float32)
+    diagonal = iota((rows, 128), 0) == iota((rows, 128), 1)
+
+    def as_row(column):
+        return jnp.sum(jnp.where(diagonal, column, 0.0), axis=0, keepdims=True)
+
+    def as_column(row):
+        return jnp.sum(jnp.where(diagonal, row, 0.0), axis=1, keepdims=True)
+
+    sums = as_row(jnp.sum(widened, axis=1, keepdims=True))
+    squares = as_row(jnp.sum(widened * widened, axis=1, keepdims=True))
+    line = iota((8, 128), 0)
+    stats[me] = jnp.where(line == 0, sums, jnp.where(line == 1, squares, 0.0))
+
+    pl.semaphore_wait(barrier, WIDE - 1)
+
+    def stat_copy(k):
+        return remote(
+            stats.at[me], stats.at[me], stat_send.at[k], stat_recv.at[me], (me + k) % WIDE
+        )
+
+    def stat_start(k, carry):
+        stat_copy(k).start()
+        return carry
+
+    lax.fori_loop(1, WIDE, stat_start, 0)
+
+    def own_copy(send_sem, target):
+        return remote(tokens, shards.at[me], send_sem, recv1.at[me], target)
+
+    @pl.when(z < Z - 1)
+    def _():
+        own_copy(send_z.at[0], index(z + 1, y, c)).start()
+
+    @pl.when(z > 0)
+    def _():
+        own_copy(send_z.at[1], index(z - 1, y, c)).start()
+
+    own_copy(send_y.at[0], y_peer).start()
+    own_copy(send_c.at[0], c_peer).start()
+
+    def shard_copy(owner, send_sem, target):
+        return remote(shards.at[owner], shards.at[owner], send_sem, recv1.at[owner], target)
+
+    def next_z(zz):
+        return z + jnp.where(zz > z, -1, 1)
+
+    def can_go(zz):
+        after = next_z(zz)
+        return jnp.logical_and(after >= 0, after < Z)
+
+    def arrival(owner):
+        shard_copy(owner, send_z.at[0], c_peer).wait_recv()
+
+    shards[me] = tokens[...]
+    acc[...] = jnp.zeros_like(acc)
+
+    def stat_wait(k, carry):
+        j = (me + k) % WIDE
+        remote(stats.at[j], stats.at[j], stat_send.at[k], stat_recv.at[j], j).wait_recv()
+        return carry
+
+    lax.fori_loop(1, WIDE, stat_wait, 0)
+    whole = jnp.sum(stats[...], axis=0)
+    features = float(depth * WIDE)
+    center = as_column(whole[0:1]) / features
+    spread = as_column(whole[1:2]) / features - center * center
+    columns[0] = jnp.broadcast_to(center, (rows, 128))
+    columns[1] = jnp.broadcast_to(lax.rsqrt(spread + norm_eps), (rows, 128))
+
+    def project(owner):
+        load_in(owner).wait()
+        x = shards[owner].astype(jnp.float32)
+        normed = (x - columns[0][:, 0:1]) * columns[1][:, 0:1] * gain[owner]
+        acc[:, 0:width] += dot(normed.astype(jnp.bfloat16), w_in[owner])
+
+    def round1(p, carry):
+        @pl.when(jnp.logical_and(p >= 1, p <= 3))
+        def _():
+            zz = z_at(p)
+            owner = index(zz, y, c)
+            arrival(owner)
+
+            @pl.when(can_go(zz))
+            def _():
+                shard_copy(owner, send_z.at[1 + p], index(next_z(zz), y, c)).start()
+
+            shard_copy(owner, send_y.at[p], y_peer).start()
+            shard_copy(owner, send_c.at[p], c_peer).start()
+
+        @pl.when(p >= 1)
+        def _():
+            owner = index(z_at(p - 1), 1 - y, c)
+            arrival(owner)
+            shard_copy(owner, send_c.at[3 + p], c_peer).start()
+
+        @pl.when(p == 2)
+        def _():
+            load_keys.start()
+            load_values.start()
+
+            def body(g, inner):
+                load_last(g).start()
+                return inner
+
+            lax.fori_loop(0, SLOTS, body, 0)
+
+        def part(i, inner):
+            late = i // 2
+            zz = z_at(p - late)
+
+            @pl.when(jnp.logical_and(p - late >= 0, p - late <= 3))
+            def _():
+                owner = index(zz, (y + late) % Y, (c + i) % C)
+
+                @pl.when(i % 2 == 1)
+                def _():
+                    arrival(owner)
+
+                project(owner)
+
+            return inner
+
+        return lax.fori_loop(0, 4, part, carry)
+
+    lax.fori_loop(0, 5, round1, 0)
+
+    offset = (width * me) % 256
+    shifted = pltpu.roll(acc[...], offset, 1).astype(jnp.bfloat16)
+    row = iota((WIDE * 16, rows), 0)
+    token = ((row >> 1) & 1) * seqs + 2 * (row >> 4) + (row & 1)
+    chosen = iota((WIDE * 16, rows), 1) == token
+    sending = jnp.zeros((WIDE * 16, 256), jnp.float32)
+    for hh in range(GROUP):
+        sending += dot(
+            pick(jnp.logical_and(chosen, ((row >> 2) & 3) == hh)),
+            shifted[:, hh * 256 : (hh + 1) * 256],
+        )
+    to_send[...] = sending.astype(jnp.bfloat16).reshape(to_send.shape)
+
+    def all_copy(k):
+        t = (me + k) % WIDE
+        return remote(to_send.at[t], arrived.at[me], all_send.at[k], all_recv.at[me], t)
+
+    def all_start(k, carry):
+        all_copy(k).start()
+        return carry
+
+    lax.fori_loop(1, WIDE, all_start, 0)
+    arrived[me] = to_send[me]
+    load_keys.wait()
+    load_values.wait()
+
+    def all_wait(k, carry):
+        j = (me + k) % WIDE
+        remote(to_send.at[j], arrived.at[j], all_send.at[k], all_recv.at[j], j).wait_recv()
+        return carry
+
+    lax.fori_loop(1, WIDE, all_wait, 0)
+
+    blocks = arrived[...].reshape(WIDE * 16, 256)
+    query_rows = 2 * heads
+    col = iota((query_rows + 16, WIDE * 16), 1)
+    head = ((width * (col >> 4)) >> 8) + ((col >> 2) & 3)
+    step = (col >> 1) & 1
+    target = jnp.where(
+        head < heads, step * heads + head, query_rows + 8 * (head - heads) + step
+    )
+    placed = iota((query_rows + 16, WIDE * 16), 0) == target
+    scale = 1.0 / math.sqrt(256)
+    slots = keys.shape[1]
+    sending = jnp.zeros((4 * heads, 256), jnp.float32)
+    for n in range(2):
+        mine = dot(pick(jnp.logical_and(placed, (col & 1) == n)), blocks)
+
+        def turn(block, cosine, sine_table):
+            first, second = block[:, 0:128], block[:, 128:256]
+            return jnp.concatenate(
+                [first * cosine - second * sine_table, second * cosine + first * sine_table],
+                axis=1,
+            ).astype(jnp.bfloat16)
+
+        def by_step(table, count, half):
+            at = iota((count, 128), 0)
+            return jnp.where(at < half, table[n : n + 1, :], table[n + 2 : n + 3, :])
+
+        query = turn(
+            mine[0:query_rows],
+            by_step(cos_ref, query_rows, heads),
+            by_step(sin_ref, query_rows, heads),
+        )
+        key_new = turn(
+            mine[query_rows : query_rows + 8], by_step(cos_ref, 8, 1), by_step(sin_ref, 8, 1)
+        )
+        value_new = mine[query_rows + 8 : query_rows + 16].astype(jnp.bfloat16)
+        scores = dot_t(query, keys[n]) * scale
+        scores = jnp.where(iota((query_rows, slots), 1) < lengths[n], scores, -1e30)
+        fresh = dot_t(query, key_new) * scale
+        t = iota((query_rows, 8), 1)
+        s = jnp.where(iota((query_rows, 8), 0) >= heads, 1, 0)
+        fresh = jnp.where(t <= s, fresh, -1e30)
+        top = jnp.maximum(
+            jnp.max(scores, axis=1, keepdims=True), jnp.max(fresh, axis=1, keepdims=True)
+        )
+        scores = jnp.exp(scores - top)
+        fresh = jnp.exp(fresh - top)
+        denom = jnp.sum(scores, axis=1, keepdims=True) + jnp.sum(fresh, axis=1, keepdims=True)
+        inverse = 1.0 / denom
+        mixed = dot((scores * inverse).astype(jnp.bfloat16), values[n])
+        mixed += dot((fresh * inverse).astype(jnp.bfloat16), value_new)
+        at = iota((4 * heads, query_rows), 0)
+        from_row = ((at >> 1) & 1) * heads + (at >> 2)
+        sending += dot(
+            pick(
+                jnp.logical_and(
+                    iota((4 * heads, query_rows), 1) == from_row, (at & 1) == n
+                )
+            ),
+            mixed.astype(jnp.bfloat16),
+        )
+    gathered[me] = sending.astype(jnp.bfloat16)
+
+    high = gathered.shape[1] // PIECES
+
+    def piece_copy(owner, q, send_sem, target):
+        part = gathered.at[owner, pl.ds(pl.multiple_of(q * high, high), high)]
+        return remote(part, part, send_sem, recv2.at[q, owner], target)
+
+    def piece_start(q, carry):
+        @pl.when(z < Z - 1)
+        def _():
+            piece_copy(me, q, send2_z.at[q, 0], index(z + 1, y, c)).start()
+
+        @pl.when(z > 0)
+        def _():
+            piece_copy(me, q, send2_z.at[q, 1], index(z - 1, y, c)).start()
+
+        piece_copy(me, q, send2_y.at[q, 0], y_peer).start()
+        piece_copy(me, q, send2_c.at[q, 0], c_peer).start()
+        return carry
+
+    lax.fori_loop(0, PIECES, piece_start, 0)
+
+    def piece_arrival(owner, q):
+        piece_copy(owner, q, send2_z.at[q, 0], c_peer).wait_recv()
+
+    def forward(q, p):
+        @pl.when(p <= 3)
+        def _():
+            zz = z_at(p)
+            owner = index(zz, y, c)
+            piece_arrival(owner, q)
+
+            @pl.when(can_go(zz))
+            def _():
+                piece_copy(owner, q, send2_z.at[q, 1 + p], index(next_z(zz), y, c)).start()
+
+            piece_copy(owner, q, send2_y.at[q, p], y_peer).start()
+            piece_copy(owner, q, send2_c.at[q, p], c_peer).start()
+
+        owner = index(z_at(p - 1), 1 - y, c)
+        piece_arrival(owner, q)
+        piece_copy(owner, q, send2_c.at[q, 3 + p], c_peer).start()
+
+        @pl.when(p == 4)
+        def _():
+            def body(j, inner):
+                piece_arrival(index(z_at(j // 2), (y + j) % Y, 1 - c), q)
+                return inner
+
+            lax.fori_loop(0, 8, body, 0)
+
+    def forward_loop(p, carry):
+        forward(0, p)
+        return carry
+
+    lax.fori_loop(1, 5, forward_loop, 0)
+
+    total[...] = jnp.zeros_like(total)
+    per_piece = groups // PIECES
+    i = iota((rows * GROUP, WIDE * 16), 0)
+    m = i % rows
+    b = m % seqs
+    source = (b >> 1) * 16 + (i // rows) * 4 + (m // seqs) * 2 + (b & 1)
+    reorder = pick(iota((rows * GROUP, WIDE * 16), 1) == source)
+
+    def multiply(g, carry):
+        q = g // per_piece
+        r = g % per_piece
+
+        @pl.when(q < PIECES - 1)
+        def _():
+            def body(p, inner):
+                forward(q + 1, p)
+                return inner
+
+            lax.fori_loop(
+                1 + (4 * r) // per_piece, 1 + (4 * r + 4) // per_piece, body, 0
+            )
+
+        load_last(g).wait()
+        block = gathered[:, pl.ds(pl.multiple_of(g * 16, 16), 16), :].reshape(WIDE * 16, 256)
+        ordered = dot(reorder, block).astype(jnp.bfloat16)
+        lined = jnp.concatenate(
+            [ordered[h * rows : (h + 1) * rows] for h in range(GROUP)], axis=1
+        )
+        total[...] += dot(lined, w_last[g % SLOTS])
+
+        @pl.when(g + SLOTS < groups)
+        def _():
+            load_last(g + SLOTS).start()
+
+        return carry
+
+    lax.fori_loop(0, groups, multiply, 0)
+    out[...] = total[...].astype(jnp.bfloat16)
+
+    def sent(k, carry):
+        stat_copy(k).wait_send()
+        all_copy(k).wait_send()
+        return carry
+
+    lax.fori_loop(1, WIDE, sent, 0)
+
+    @pl.when(z < Z - 1)
+    def _():
+        own_copy(send_z.at[0], index(z + 1, y, c)).wait_send()
+
+    @pl.when(z > 0)
+    def _():
+        own_copy(send_z.at[1], index(z - 1, y, c)).wait_send()
+
+    own_copy(send_y.at[0], y_peer).wait_send()
+    own_copy(send_c.at[0], c_peer).wait_send()
+
+    def sent1(p, carry):
+        @pl.when(p <= 3)
+        def _():
+            zz = z_at(p)
+            owner = index(zz, y, c)
+
+            @pl.when(can_go(zz))
+            def _():
+                shard_copy(owner, send_z.at[1 + p], index(next_z(zz), y, c)).wait_send()
+
+            shard_copy(owner, send_y.at[p], y_peer).wait_send()
+            shard_copy(owner, send_c.at[p], c_peer).wait_send()
+
+        shard_copy(index(z_at(p - 1), 1 - y, c), send_c.at[3 + p], c_peer).wait_send()
+        return carry
+
+    lax.fori_loop(1, 5, sent1, 0)
+
+    def sent2(q, carry):
+        @pl.when(z < Z - 1)
+        def _():
+            piece_copy(me, q, send2_z.at[q, 0], index(z + 1, y, c)).wait_send()
+
+        @pl.when(z > 0)
+        def _():
+            piece_copy(me, q, send2_z.at[q, 1], index(z - 1, y, c)).wait_send()
+
+        piece_copy(me, q, send2_y.at[q, 0], y_peer).wait_send()
+        piece_copy(me, q, send2_c.at[q, 0], c_peer).wait_send()
+
+        def body(p, inner):
+            @pl.when(p <= 3)
+            def _():
+                zz = z_at(p)
+                owner = index(zz, y, c)
+
+                @pl.when(can_go(zz))
+                def _():
+                    piece_copy(
+                        owner, q, send2_z.at[q, 1 + p], index(next_z(zz), y, c)
+                    ).wait_send()
+
+                piece_copy(owner, q, send2_y.at[q, p], y_peer).wait_send()
+                piece_copy(owner, q, send2_c.at[q, p], c_peer).wait_send()
+
+            piece_copy(
+                index(z_at(p - 1), 1 - y, c), q, send2_c.at[q, 3 + p], c_peer
+            ).wait_send()
+            return inner
+
+        return lax.fori_loop(1, 5, body, carry)
+
+    lax.fori_loop(0, PIECES, sent2, 0)
+
+
+def fused(tokens, norm_gain, w_qkv, w_out, cache_k, cache_v, lengths):
+    step_count, seqs, depth = tokens.shape
+    rows = step_count * seqs
+    inner, out_width = w_out.shape
+    head_dim = cache_k.shape[2]
+    heads = inner // head_dim
+    half = head_dim // 2
+    freqs = jnp.exp(jnp.arange(half, dtype=jnp.float32) * (-2.0 * math.log(10000.0) / head_dim))
+    positions = lengths[None, :] + jnp.arange(step_count, dtype=jnp.int32)[:, None]
+    angles = positions.reshape(-1).astype(jnp.float32)[:, None] * freqs
+    vmem = pl.BlockSpec(memory_space=pltpu.VMEM)
+    anywhere = pl.BlockSpec(memory_space=pl.ANY)
+    dma = pltpu.SemaphoreType.DMA
+    result = pl.pallas_call(
+        fused_kernel,
+        out_shape=jax.ShapeDtypeStruct((rows, out_width), jnp.bfloat16),
+        in_specs=[pl.BlockSpec(memory_space=pltpu.SMEM)] + [vmem] * 4 + [anywhere] * 4,
+        out_specs=vmem,
+        scratch_shapes=[
+            pltpu.VMEM((WIDE, rows, depth), jnp.bfloat16),
+            pltpu.VMEM((WIDE, 8, 128), jnp.float32),
+            pltpu.VMEM((WIDE, depth, w_qkv.shape[1]), jnp.bfloat16),
+            pltpu.VMEM((SLOTS, GROUP * head_dim, out_width), jnp.bfloat16),
+            pltpu.VMEM(cache_k.shape, jnp.bfloat16),
+            pltpu.VMEM(cache_v.shape, jnp.bfloat16),
+            pltpu.VMEM((rows, GROUP * head_dim), jnp.float32),
+            pltpu.VMEM((WIDE, 16, head_dim), jnp.bfloat16),
+            pltpu.VMEM((WIDE, 16, head_dim), jnp.bfloat16),
+            pltpu.VMEM((WIDE, 4 * heads, head_dim), jnp.bfloat16),
+            pltpu.VMEM((rows, out_width), jnp.float32),
+            pltpu.VMEM((2, rows, 128), jnp.float32),
+            dma((WIDE,)),
+            dma((heads // GROUP,)),
+            dma((2,)),
+            dma((WIDE,)),
+            dma((WIDE,)),
+            dma((5,)),
+            dma((4,)),
+            dma((8,)),
+            dma((WIDE,)),
+            dma((WIDE,)),
+            dma((WIDE,)),
+            dma((PIECES, 5)),
+            dma((PIECES, 4)),
+            dma((PIECES, 8)),
+            dma((PIECES, WIDE)),
+        ],
+        compiler_params=pltpu.CompilerParams(
+            collective_id=0, has_side_effects=True, vmem_limit_bytes=62 * 1024 * 1024
+        ),
+    )(
+        lengths,
+        tokens.reshape(rows, depth),
+        norm_gain.reshape(WIDE, 1, depth),
+        jnp.cos(angles),
+        jnp.sin(angles),
+        w_qkv,
+        w_out,
+        cache_k,
+        cache_v,
+    )
+    return result.reshape(step_count, seqs, out_width)
+
+
 def solution(mesh):
     placed = (
         P(None, "groups", "wide"),
@@ -91,5 +685,5 @@
         P(("groups", "wide")),
     )
     return jax.shard_map(
-        on_device, mesh=mesh, in_specs=placed, out_specs=P(None, "groups", "wide"), check_vma=False
-    )
+        fused if mesh.shape["wide"] == WIDE else on_device, mesh=mesh, in_specs=placed, out_specs=P(None, "groups", "wide"), check_vma=False
+    )

time: 147 us -> 121 us (0.82); the launches traced: 147 us -> 119 us
  waiting for transfers between devices: 92.4 us -> 0 us
  Pallas kernels: 0 us -> 78.8 us
  local copies, waits for them, and re-layouts: 1.81 us -> 39.1 us
  matrix products: 31.5 us -> 0 us
  between operations: 13.5 us -> 0.01 us
  starting transfers between devices: 3.57 us -> 0 us
  other arithmetic: 4.07 us -> 1.37 us
    all_gather x2 -> x0, waiting for transfers between devices: 84.1 us -> none  [the longest x1 46.7 us: on_device(): gathered = lax.all_gather(tokens, 'wide', axis=2, tiled=True)]
    pallas_call x0 -> x1, Pallas kernels: none -> 78.8 us  [fused(): pl.pallas_call(fused_kernel, out_shape=jax.ShapeDtypeStruct((rows, out_wi...]
    unnamed x12 -> x2, local copies, waits for them, and re-layouts: 0.03 us -> 39 us
    dot_general x6 -> x0, matrix products: 31.5 us -> none  [the longest x1 15.8 us: on_device(): jnp.einsum('snh,hd->snd', lax.all_gather(mixed, 'wide', axis=1, tiled=Tru...]
    all_to_all x1 -> x0, waiting for transfers between devices: 7.54 us -> none  [on_device(): lax.all_to_all(projected, 'wide', split_axis=1, concat_axis=2, tiled=True)]
    all_to_all x1 -> x0, starting transfers between devices: 3.53 us -> none  [on_device(): lax.all_to_all(projected, 'wide', split_axis=1, concat_axis=2, tiled=True)]
    reduce_sum x3 -> x0, other arithmetic: 3 us -> none  [the longest x1 2.6 us: on_device(): center = jnp.mean(widened, axis=-1, keepdims=True)]
  transfers between devices with their start and end apart: 3 -> 0, of which waited for: 3 -> 0; matrix products, arithmetic and copies ran while one was open for 1% -> 0% of each run, Pallas kernels for 0% -> 0%
where the time goes in v1:
time: 121 us; the launch traced here: 119 us
  Pallas kernels  78.8 us (65%)
  local copies, waits for them, and re-layouts  39.1 us (32%)
  other arithmetic  1.37 us (1%)
    pallas_call x1, Pallas kernels, fused(): pl.pallas_call(fused_kernel, out_shape=jax.ShapeDtypeStruct((rows, out_wi...  78.8 us
    unnamed x2, local copies, waits for them, and re-layouts  39 us

profile of v1, /device:TPU:0, one launch (start us, length us, event | category | flops | bytes accessed | tf_op | source)
XLA Modules:
  0.0 119.3 jit_solution(11577536151810450183)
XLA Ops:
  0.0 0.7 add_convert_fusion
  0.7 0.1 convert_element_type.11
  0.8 0.7 multiply_sine_fusion
  1.5 37.4 %copy.8.w_qkv = bf16[18432,800]{1,0:T(8,128)(2,1)} copy(bf16[18432,800]{0,1:T(8,128)(2,1)} %param.9) | data formatting | bytes 58982400 | tf_op args[2]
  38.9 78.8 %shard_map.73 = bf16[64,1152]{1,0:T(8,128)(2,1)} custom-call(s32[2]{0:T(128)} %lengths.1, bf16[64,1152]{1,0:T(8,128)(2,1)} %bitcast.4, f32[16,1,1152]{2,1,0:T(1,128)} %bitcast.5, f32[4,128]{1,0:T(4,128)} %get-tuple-element.6.cos_ref, f32[4,128]{1,0:T(4,128)} %get-tuple-element.5.sin_ref, bf16[18432,800]{1,0:T(8,128)(2,1)} %copy.8.w_qkv, ...), custom_call_target="tpu_custom_call" | custom-call | tf_op jit(solution)/shard_map/pallas_call | solution.py:626
  117.7 1.6 %copy.10 = bf16[2,32,1152]{2,1,0:T(8,128)(2,1)} copy(bf16[2,32,1152]{2,1,0:T(8,128)(2,1)} %bitcast.3) | data formatting | bytes 294912
  (1 shorter events, 0.0 us)

commit v2 on v1

--- a/solution.py
+++ b/solution.py
@@ -14,6 +14,7 @@
 WIDE = Z * Y * C
 SLOTS = 8
 PIECES = 4
+HALVES = 2
 GROUP = 4
 
 
@@ -109,8 +110,6 @@
     lengths,
     tokens,
     gain,
-    cos_ref,
-    sin_ref,
     w_qkv,
     w_out,
     cache_k,
@@ -133,16 +132,13 @@
     cache_sem,
     stat_send,
     stat_recv,
-    send_z,
-    send_y,
-    send_c,
+    send1,
     recv1,
     all_send,
     all_recv,
-    send2_z,
-    send2_y,
-    send2_c,
+    send2,
     recv2,
+    angles,
 ):
     me = lax.axis_index("wide")
     z = me // (Y * C)
@@ -152,7 +148,7 @@
     rows = tokens.shape[0]
     seqs = rows // 2
     out_depth = w_last.shape[1]
-    width = w_qkv.shape[1]
+    width = w_qkv.shape[0]
     heads = w_out.shape[0] // 256
     groups = heads // GROUP
     mirrored = (z + z // 2) % 2
@@ -180,7 +176,7 @@
 
     def load_in(owner):
         return pltpu.make_async_copy(
-            w_qkv.at[pl.ds(pl.multiple_of(owner * depth, depth), depth)],
+            w_qkv.at[:, pl.ds(pl.multiple_of(owner * depth, depth), depth)],
             w_in.at[owner],
             local_sem.at[owner],
         )
@@ -247,33 +243,40 @@
 
     lax.fori_loop(1, WIDE, stat_start, 0)
 
-    def own_copy(send_sem, target):
-        return remote(tokens, shards.at[me], send_sem, recv1.at[me], target)
-
-    @pl.when(z < Z - 1)
-    def _():
-        own_copy(send_z.at[0], index(z + 1, y, c)).start()
-
-    @pl.when(z > 0)
-    def _():
-        own_copy(send_z.at[1], index(z - 1, y, c)).start()
-
-    own_copy(send_y.at[0], y_peer).start()
-    own_copy(send_c.at[0], c_peer).start()
-
-    def shard_copy(owner, send_sem, target):
-        return remote(shards.at[owner], shards.at[owner], send_sem, recv1.at[owner], target)
-
-    def next_z(zz):
-        return z + jnp.where(zz > z, -1, 1)
-
-    def can_go(zz):
-        after = next_z(zz)
-        return jnp.logical_and(after >= 0, after < Z)
-
-    def arrival(owner):
-        shard_copy(owner, send_z.at[0], c_peer).wait_recv()
-
+    share = rows // HALVES
+
+    def shard_copy(owner, h, k, target):
+        part = shards.at[owner, pl.ds(pl.multiple_of(h * share, share), share)]
+        return remote(part, part, send1.at[h, k], recv1.at[h, owner], target)
+
+    def own_copy(h, k, target):
+        part = tokens.at[pl.ds(pl.multiple_of(h * share, share), share)]
+        there = shards.at[me, pl.ds(pl.multiple_of(h * share, share), share)]
+        return remote(part, there, send1.at[h, k], recv1.at[h, me], target)
+
+    def own_start(h, carry):
+        own_copy(h, 3, y_peer).start()
+        own_copy(h, 7, c_peer).start()
+        return carry
+
+    lax.fori_loop(0, HALVES, own_start, 0)
+
+    def own_z_start(j, carry):
+        p = 1 + j // HALVES
+        own_copy(j % HALVES, p - 1, index(z_at(p), y, c)).start()
+        return carry
+
+    lax.fori_loop(0, 3 * HALVES, own_z_start, 0)
+
+    def arrival(owner, h):
+        shard_copy(owner, h, 0, c_peer).wait_recv()
+
+    freqs = jnp.exp(iota((8, 128), 1).astype(jnp.float32) * (-2.0 * math.log(10000.0) / 256))
+    line = iota((8, 128), 0)
+    position = jnp.where((line & 1) == 0, lengths[0], lengths[1]) + ((line >> 1) & 1)
+    angle = position.astype(jnp.float32) * freqs
+    angles[0] = jnp.cos(angle)
+    angles[1] = jnp.sin(angle)
     shards[me] = tokens[...]
     acc[...] = jnp.zeros_like(acc)
 
@@ -294,27 +297,31 @@
         load_in(owner).wait()
         x = shards[owner].astype(jnp.float32)
         normed = (x - columns[0][:, 0:1]) * columns[1][:, 0:1] * gain[owner]
-        acc[:, 0:width] += dot(normed.astype(jnp.bfloat16), w_in[owner])
+        acc[:, 0:width] += dot_t(normed.astype(jnp.bfloat16), w_in[owner])
 
     def round1(p, carry):
-        @pl.when(jnp.logical_and(p >= 1, p <= 3))
-        def _():
-            zz = z_at(p)
-            owner = index(zz, y, c)
-            arrival(owner)
-
-            @pl.when(can_go(zz))
+        def take(h, inner):
+            @pl.when(jnp.logical_and(p >= 1, p <= 3))
             def _():
-                shard_copy(owner, send_z.at[1 + p], index(next_z(zz), y, c)).start()
-
-            shard_copy(owner, send_y.at[p], y_peer).start()
-            shard_copy(owner, send_c.at[p], c_peer).start()
-
-        @pl.when(p >= 1)
-        def _():
-            owner = index(z_at(p - 1), 1 - y, c)
-            arrival(owner)
-            shard_copy(owner, send_c.at[3 + p], c_peer).start()
+                owner = index(z_at(p), y, c)
+                arrival(owner, h)
+                shard_copy(owner, h, 3 + p, y_peer).start()
+                shard_copy(owner, h, 7 + p, c_peer).start()
+
+            return inner
+
+        lax.fori_loop(0, HALVES, take, 0)
+
+        def take_y(h, inner):
+            @pl.when(p >= 1)
+            def _():
+                owner = index(z_at(p - 1), 1 - y, c)
+                arrival(owner, h)
+                shard_copy(owner, h, 10 + p, c_peer).start()
+
+            return inner
+
+        lax.fori_loop(0, HALVES, take_y, 0)
 
         @pl.when(p == 2)
         def _():
@@ -337,7 +344,11 @@
 
                 @pl.when(i % 2 == 1)
                 def _():
-                    arrival(owner)
+                    def body(h, deep):
+                        arrival(owner, h)
+                        return deep
+
+                    lax.fori_loop(0, HALVES, body, 0)
 
                 project(owner)
 
@@ -408,11 +419,11 @@
 
         query = turn(
             mine[0:query_rows],
-            by_step(cos_ref, query_rows, heads),
-            by_step(sin_ref, query_rows, heads),
+            by_step(angles[0], query_rows, heads),
+            by_step(angles[1], query_rows, heads),
         )
         key_new = turn(
-            mine[query_rows : query_rows + 8], by_step(cos_ref, 8, 1), by_step(sin_ref, 8, 1)
+            mine[query_rows : query_rows + 8], by_step(angles[0], 8, 1), by_step(angles[1], 8, 1)
         )
         value_new = mine[query_rows + 8 : query_rows + 16].astype(jnp.bfloat16)
         scores = dot_t(query, keys[n]) * scale
@@ -444,59 +455,56 @@
 
     high = gathered.shape[1] // PIECES
 
-    def piece_copy(owner, q, send_sem, target):
+    def piece_copy(owner, q, k, target):
         part = gathered.at[owner, pl.ds(pl.multiple_of(q * high, high), high)]
-        return remote(part, part, send_sem, recv2.at[q, owner], target)
+        return remote(part, part, send2.at[q, k], recv2.at[q, owner], target)
 
     def piece_start(q, carry):
-        @pl.when(z < Z - 1)
-        def _():
-            piece_copy(me, q, send2_z.at[q, 0], index(z + 1, y, c)).start()
-
-        @pl.when(z > 0)
-        def _():
-            piece_copy(me, q, send2_z.at[q, 1], index(z - 1, y, c)).start()
-
-        piece_copy(me, q, send2_y.at[q, 0], y_peer).start()
-        piece_copy(me, q, send2_c.at[q, 0], c_peer).start()
-        return carry
+        piece_copy(me, q, 3, y_peer).start()
+        piece_copy(me, q, 7, c_peer).start()
+
+        def body(p, inner):
+            piece_copy(me, q, p - 1, index(z_at(p), y, c)).start()
+            return inner
+
+        return lax.fori_loop(1, 4, body, carry)
 
     lax.fori_loop(0, PIECES, piece_start, 0)
 
     def piece_arrival(owner, q):
-        piece_copy(owner, q, send2_z.at[q, 0], c_peer).wait_recv()
+        piece_copy(owner, q, 0, c_peer).wait_recv()
 
     def forward(q, p):
-        @pl.when(p <= 3)
-        def _():
-            zz = z_at(p)
-            owner = index(zz, y, c)
-            piece_arrival(owner, q)
-
-            @pl.when(can_go(zz))
-            def _():
-                piece_copy(owner, q, send2_z.at[q, 1 + p], index(next_z(zz), y, c)).start()
-
-            piece_copy(owner, q, send2_y.at[q, p], y_peer).start()
-            piece_copy(owner, q, send2_c.at[q, p], c_peer).start()
-
-        owner = index(z_at(p - 1), 1 - y, c)
+        owner = index(z_at(p), y, c)
         piece_arrival(owner, q)
-        piece_copy(owner, q, send2_c.at[q, 3 + p], c_peer).start()
-
-        @pl.when(p == 4)
-        def _():
-            def body(j, inner):
-                piece_arrival(index(z_at(j // 2), (y + j) % Y, 1 - c), q)
-                return inner
-
-            lax.fori_loop(0, 8, body, 0)
-
-    def forward_loop(p, carry):
-        forward(0, p)
-        return carry
-
-    lax.fori_loop(1, 5, forward_loop, 0)
+        piece_copy(owner, q, 3 + p, y_peer).start()
+        piece_copy(owner, q, 7 + p, c_peer).start()
+
+    def forward_y(q, p):
+        owner = index(z_at(p), 1 - y, c)
+        piece_arrival(owner, q)
+        piece_copy(owner, q, 11 + p, c_peer).start()
+
+    def stage_a(q):
+        def body(p, inner):
+            forward(q, p)
+            return inner
+
+        lax.fori_loop(1, 4, body, 0)
+
+    def stage_b(q):
+        def body(p, inner):
+            forward_y(q, p)
+            return inner
+
+        lax.fori_loop(0, 4, body, 0)
+
+    def stage_c(q):
+        def body(j, inner):
+            piece_arrival(index(z_at(j // 2), (y + j) % Y, 1 - c), q)
+            return inner
+
+        lax.fori_loop(0, 8, body, 0)
 
     total[...] = jnp.zeros_like(total)
     per_piece = groups // PIECES
@@ -507,18 +515,19 @@
     reorder = pick(iota((rows * GROUP, WIDE * 16), 1) == source)
 
     def multiply(g, carry):
-        q = g // per_piece
-        r = g % per_piece
-
-        @pl.when(q < PIECES - 1)
+        @pl.when(g % per_piece == 0)
         def _():
-            def body(p, inner):
-                forward(q + 1, p)
-                return inner
-
-            lax.fori_loop(
-                1 + (4 * r) // per_piece, 1 + (4 * r + 4) // per_piece, body, 0
-            )
+            q = g // per_piece
+
+            @pl.when(q < PIECES - 2)
+            def _():
+                stage_a(q + 2)
+
+            @pl.when(q < PIECES - 1)
+            def _():
+                stage_b(q + 1)
+
+            stage_c(q)
 
         load_last(g).wait()
         block = gathered[:, pl.ds(pl.multiple_of(g * 16, 16), 16), :].reshape(WIDE * 16, 256)
@@ -534,6 +543,9 @@
 
         return carry
 
+    stage_a(0)
+    stage_a(1)
+    stage_b(0)
     lax.fori_loop(0, groups, multiply, 0)
     out[...] = total[...].astype(jnp.bfloat16)
 
@@ -544,70 +556,23 @@
 
     lax.fori_loop(1, WIDE, sent, 0)
 
-    @pl.when(z < Z - 1)
-    def _():
-        own_copy(send_z.at[0], index(z + 1, y, c)).wait_send()
-
-    @pl.when(z > 0)
-    def _():
-        own_copy(send_z.at[1], index(z - 1, y, c)).wait_send()
-
-    own_copy(send_y.at[0], y_peer).wait_send()
-    own_copy(send_c.at[0], c_peer).wait_send()
-
-    def sent1(p, carry):
-        @pl.when(p <= 3)
-        def _():
-            zz = z_at(p)
-            owner = index(zz, y, c)
-
-            @pl.when(can_go(zz))
-            def _():
-                shard_copy(owner, send_z.at[1 + p], index(next_z(zz), y, c)).wait_send()
-
-            shard_copy(owner, send_y.at[p], y_peer).wait_send()
-            shard_copy(owner, send_c.at[p], c_peer).wait_send()
-
-        shard_copy(index(z_at(p - 1), 1 - y, c), send_c.at[3 + p], c_peer).wait_send()
-        return carry
-
-    lax.fori_loop(1, 5, sent1, 0)
-
-    def sent2(q, carry):
-        @pl.when(z < Z - 1)
-        def _():
-            piece_copy(me, q, send2_z.at[q, 0], index(z + 1, y, c)).wait_send()
-
-        @pl.when(z > 0)
-        def _():
-            piece_copy(me, q, send2_z.at[q, 1], index(z - 1, y, c)).wait_send()
-
-        piece_copy(me, q, send2_y.at[q, 0], y_peer).wait_send()
-        piece_copy(me, q, send2_c.at[q, 0], c_peer).wait_send()
-
-        def body(p, inner):
-            @pl.when(p <= 3)
-            def _():
-                zz = z_at(p)
-                owner = index(zz, y, c)
-
-                @pl.when(can_go(zz))
-                def _():
-                    piece_copy(
-                        owner, q, send2_z.at[q, 1 + p], index(next_z(zz), y, c)
-                    ).wait_send()
-
-                piece_copy(owner, q, send2_y.at[q, p], y_peer).wait_send()
-                piece_copy(owner, q, send2_c.at[q, p], c_peer).wait_send()
-
-            piece_copy(
-                index(z_at(p - 1), 1 - y, c), q, send2_c.at[q, 3 + p], c_peer
-            ).wait_send()
-            return inner
-
-        return lax.fori_loop(1, 5, body, carry)
-
-    lax.fori_loop(0, PIECES, sent2, 0)
+    def sent1(k, carry):
+        def body(h, inner):
+            own_copy(h, k, c_peer).wait_send()
+            return inner
+
+        return lax.fori_loop(0, HALVES, body, carry)
+
+    lax.fori_loop(0, 15, sent1, 0)
+
+    def sent2(k, carry):
+        def body(q, inner):
+            piece_copy(me, q, k, c_peer).wait_send()
+            return inner
+
+        return lax.fori_loop(0, PIECES, body, carry)
+
+    lax.fori_loop(0, 15, sent2, 0)
 
 
 def fused(tokens, norm_gain, w_qkv, w_out, cache_k, cache_v, lengths):
@@ -616,22 +581,18 @@
     inner, out_width = w_out.shape
     head_dim = cache_k.shape[2]
     heads = inner // head_dim
-    half = head_dim // 2
-    freqs = jnp.exp(jnp.arange(half, dtype=jnp.float32) * (-2.0 * math.log(10000.0) / head_dim))
-    positions = lengths[None, :] + jnp.arange(step_count, dtype=jnp.int32)[:, None]
-    angles = positions.reshape(-1).astype(jnp.float32)[:, None] * freqs
     vmem = pl.BlockSpec(memory_space=pltpu.VMEM)
     anywhere = pl.BlockSpec(memory_space=pl.ANY)
     dma = pltpu.SemaphoreType.DMA
     result = pl.pallas_call(
         fused_kernel,
         out_shape=jax.ShapeDtypeStruct((rows, out_width), jnp.bfloat16),
-        in_specs=[pl.BlockSpec(memory_space=pltpu.SMEM)] + [vmem] * 4 + [anywhere] * 4,
+        in_specs=[pl.BlockSpec(memory_space=pltpu.SMEM)] + [vmem] * 2 + [anywhere] * 4,
         out_specs=vmem,
         scratch_shapes=[
             pltpu.VMEM((WIDE, rows, depth), jnp.bfloat16),
             pltpu.VMEM((WIDE, 8, 128), jnp.float32),
-            pltpu.VMEM((WIDE, depth, w_qkv.shape[1]), jnp.bfloat16),
+            pltpu.VMEM((WIDE, w_qkv.shape[1], depth), jnp.bfloat16),
             pltpu.VMEM((SLOTS, GROUP * head_dim, out_width), jnp.bfloat16),
             pltpu.VMEM(cache_k.shape, jnp.bfloat16),
             pltpu.VMEM(cache_v.shape, jnp.bfloat16),
@@ -646,16 +607,13 @@
             dma((2,)),
             dma((WIDE,)),
             dma((WIDE,)),
-            dma((5,)),
-            dma((4,)),
-            dma((8,)),
+            dma((HALVES, 15)),
+            dma((HALVES, WIDE)),
             dma((WIDE,)),
             dma((WIDE,)),
-            dma((WIDE,)),
-            dma((PIECES, 5)),
-            dma((PIECES, 4)),
-            dma((PIECES, 8)),
+            dma((PIECES, 15)),
             dma((PIECES, WIDE)),
+            pltpu.VMEM((2, 8, 128), jnp.float32),
         ],
         compiler_params=pltpu.CompilerParams(
             collective_id=0, has_side_effects=True, vmem_limit_bytes=62 * 1024 * 1024
@@ -664,9 +622,7 @@
         lengths,
         tokens.reshape(rows, depth),
         norm_gain.reshape(WIDE, 1, depth),
-        jnp.cos(angles),
-        jnp.sin(angles),
-        w_qkv,
+        w_qkv.T,
         w_out,
         cache_k,
         cache_v,

time: 121 us -> 67.5 us (0.56); the launches traced: 119 us -> 67.4 us
  local copies, waits for them, and re-layouts: 39.1 us -> 1.58 us
  Pallas kernels: 78.8 us -> 65.8 us
  other arithmetic: 1.37 us -> 0 us
    unnamed x2 -> x1, local copies, waits for them, and re-layouts: 39 us -> 1.58 us
    pallas_call x1, Pallas kernels: 78.8 us -> 65.8 us  [fused(): pl.pallas_call(fused_kernel, out_shape=jax.ShapeDtypeStruct((rows, out_wi...]
where the time goes in v2:
time: 67.5 us; the launch traced here: 67.4 us
  Pallas kernels  65.8 us (97%)
  local copies, waits for them, and re-layouts  1.58 us (2%)
    pallas_call x1, Pallas kernels, fused(): pl.pallas_call(fused_kernel, out_shape=jax.ShapeDtypeStruct((rows, out_wi...  65.8 us
    unnamed x1, local copies, waits for them, and re-layouts  1.58 us

profile of v2, /device:TPU:0, one launch (start us, length us, event | category | flops | bytes accessed | tf_op | source)
XLA Modules:
  0.0 67.4 jit_solution(14695003212717294570)
XLA Ops:
  0.0 65.8 %shard_map.73 = bf16[64,1152]{1,0:T(8,128)(2,1)} custom-call(s32[2]{0:T(128)} %lengths.1, bf16[64,1152]{1,0:T(8,128)(2,1)} %bitcast.6, f32[16,1,1152]{2,1,0:T(1,128)} %bitcast.7, bf16[800,18432]{1,0:T(8,128)(2,1)} %bitcast.4, bf16[12288,1152]{1,0:T(8,128)(2,1)} %w_out.1, bf16[2,2048,256]{2,1,0:T(8,128)(2,1)} %cache_k.1, bf16[2,2048,256]{2,1,0:T(8,128)(2,1)} %cache_v.1), custom_call_target="tpu_custom_call" | custom-call | tf_op jit(solution)/shard_map/pallas_call | solution.py:587
  65.8 1.6 %copy.9 = bf16[2,32,1152]{2,1,0:T(8,128)(2,1)} copy(bf16[2,32,1152]{2,1,0:T(8,128)(2,1)} %bitcast.5) | data formatting | bytes 294912

commit v3 on v2

--- a/solution.py
+++ b/solution.py
@@ -14,7 +14,7 @@
 WIDE = Z * Y * C
 SLOTS = 8
 PIECES = 4
-HALVES = 2
+HALVES = 4
 GROUP = 4
 
 
@@ -134,10 +134,12 @@
     stat_recv,
     send1,
     recv1,
+    near1,
     all_send,
     all_recv,
     send2,
     recv2,
+    near2,
     angles,
 ):
     me = lax.axis_index("wide")
@@ -174,6 +176,58 @@
     y_peer = index(z, 1 - y, c)
     c_peer = index(z, y, 1 - c)
 
+    def next_z(zz):
+        return z + jnp.where(zz > z, -1, 1)
+
+    def can_go(zz):
+        after = next_z(zz)
+        return jnp.logical_and(after >= 0, after < Z)
+
+    def send_own(copy, h):
+        @pl.when(z < Z - 1)
+        def _():
+            copy(me, h, 0, index(z + 1, y, c)).start()
+
+        @pl.when(z > 0)
+        def _():
+            copy(me, h, 0, index(z - 1, y, c)).start()
+
+        copy(me, h, 1, y_peer).start()
+        copy(me, h, 2, c_peer).start()
+
+    def pass_on(copy, h, p):
+        zz = z_at(p)
+        owner = index(zz, y, c)
+        copy(owner, h, 0, c_peer).wait_recv()
+
+        @pl.when(can_go(zz))
+        def _():
+            copy(owner, h, 0, index(next_z(zz), y, c)).start()
+
+        copy(owner, h, 1, y_peer).start()
+        copy(owner, h, 2, c_peer).start()
+
+    def pass_y(copy, h, p):
+        owner = index(z_at(p), 1 - y, c)
+        copy(owner, h, 1, c_peer).wait_recv()
+        copy(owner, h, 2, c_peer).start()
+
+    def all_sent(buffer, sems):
+        def sent(count, kind):
+            part = buffer.at[pl.ds(0, count)]
+            remote(part, part, sems.at[kind], sems.at[kind], c_peer).wait_send()
+
+        @pl.when(mirrored == 1)
+        def _():
+            sent(5, 0)
+
+        @pl.when(mirrored == 0)
+        def _():
+            sent(1, 0)
+
+        sent(4, 1)
+        sent(8, 2)
+
     def load_in(owner):
         return pltpu.make_async_copy(
             w_qkv.at[:, pl.ds(pl.multiple_of(owner * depth, depth), depth)],
@@ -234,7 +288,7 @@
 
     def stat_copy(k):
         return remote(
-            stats.at[me], stats.at[me], stat_send.at[k], stat_recv.at[me], (me + k) % WIDE
+            stats.at[me], stats.at[me], stat_send.at[0], stat_recv.at[0], (me + k) % WIDE
         )
 
     def stat_start(k, carry):
@@ -245,31 +299,23 @@
 
     share = rows // HALVES
 
+    def into(owner, h, k):
+        return near1.at[owner] if k == 2 else recv1.at[h, owner]
+
     def shard_copy(owner, h, k, target):
         part = shards.at[owner, pl.ds(pl.multiple_of(h * share, share), share)]
-        return remote(part, part, send1.at[h, k], recv1.at[h, owner], target)
-
-    def own_copy(h, k, target):
+        return remote(part, part, send1.at[k], into(owner, h, k), target)
+
+    def own_copy(owner, h, k, target):
         part = tokens.at[pl.ds(pl.multiple_of(h * share, share), share)]
         there = shards.at[me, pl.ds(pl.multiple_of(h * share, share), share)]
-        return remote(part, there, send1.at[h, k], recv1.at[h, me], target)
+        return remote(part, there, send1.at[k], into(me, h, k), target)
 
     def own_start(h, carry):
-        own_copy(h, 3, y_peer).start()
-        own_copy(h, 7, c_peer).start()
+        send_own(own_copy, h)
         return carry
 
     lax.fori_loop(0, HALVES, own_start, 0)
-
-    def own_z_start(j, carry):
-        p = 1 + j // HALVES
-        own_copy(j % HALVES, p - 1, index(z_at(p), y, c)).start()
-        return carry
-
-    lax.fori_loop(0, 3 * HALVES, own_z_start, 0)
-
-    def arrival(owner, h):
-        shard_copy(owner, h, 0, c_peer).wait_recv()
 
     freqs = jnp.exp(iota((8, 128), 1).astype(jnp.float32) * (-2.0 * math.log(10000.0) / 256))
     line = iota((8, 128), 0)
@@ -280,12 +326,8 @@
     shards[me] = tokens[...]
     acc[...] = jnp.zeros_like(acc)
 
-    def stat_wait(k, carry):
-        j = (me + k) % WIDE
-        remote(stats.at[j], stats.at[j], stat_send.at[k], stat_recv.at[j], j).wait_recv()
-        return carry
-
-    lax.fori_loop(1, WIDE, stat_wait, 0)
+    others = stats.at[pl.ds(0, WIDE - 1)]
+    remote(others, others, stat_send.at[0], stat_recv.at[0], c_peer).wait_recv()
     whole = jnp.sum(stats[...], axis=0)
     features = float(depth * WIDE)
     center = as_column(whole[0:1]) / features
@@ -300,29 +342,6 @@
         acc[:, 0:width] += dot_t(normed.astype(jnp.bfloat16), w_in[owner])
 
     def round1(p, carry):
-        def take(h, inner):
-            @pl.when(jnp.logical_and(p >= 1, p <= 3))
-            def _():
-                owner = index(z_at(p), y, c)
-                arrival(owner, h)
-                shard_copy(owner, h, 3 + p, y_peer).start()
-                shard_copy(owner, h, 7 + p, c_peer).start()
-
-            return inner
-
-        lax.fori_loop(0, HALVES, take, 0)
-
-        def take_y(h, inner):
-            @pl.when(p >= 1)
-            def _():
-                owner = index(z_at(p - 1), 1 - y, c)
-                arrival(owner, h)
-                shard_copy(owner, h, 10 + p, c_peer).start()
-
-            return inner
-
-        lax.fori_loop(0, HALVES, take_y, 0)
-
         @pl.when(p == 2)
         def _():
             load_keys.start()
@@ -335,28 +354,34 @@
             lax.fori_loop(0, SLOTS, body, 0)
 
         def part(i, inner):
-            late = i // 2
-            zz = z_at(p - late)
+            @pl.when(jnp.logical_and(p >= 1, p <= 3))
+            def _():
+                pass_on(shard_copy, i, p)
+
+            @pl.when(jnp.logical_and(p >= 1, p <= 4))
+            def _():
+                pass_y(shard_copy, i, p - 1)
+
+            late = 1 + i // 2
 
             @pl.when(jnp.logical_and(p - late >= 0, p - late <= 3))
             def _():
-                owner = index(zz, (y + late) % Y, (c + i) % C)
+                owner = index(z_at(p - late), (y + i // 2) % Y, (c + i) % C)
 
                 @pl.when(i % 2 == 1)
                 def _():
-                    def body(h, deep):
-                        arrival(owner, h)
-                        return deep
-
-                    lax.fori_loop(0, HALVES, body, 0)
+                    whole_shard = shards.at[owner]
+                    remote(
+                        whole_shard, whole_shard, send1.at[2], near1.at[owner], c_peer
+                    ).wait_recv()
 
                 project(owner)
 
             return inner
 
-        return lax.fori_loop(0, 4, part, carry)
-
-    lax.fori_loop(0, 5, round1, 0)
+        return lax.fori_loop(0, HALVES, part, carry)
+
+    lax.fori_loop(0, 6, round1, 0)
 
     offset = (width * me) % 256
     shifted = pltpu.roll(acc[...], offset, 1).astype(jnp.bfloat16)
@@ -373,7 +398,7 @@
 
     def all_copy(k):
         t = (me + k) % WIDE
-        return remote(to_send.at[t], arrived.at[me], all_send.at[k], all_recv.at[me], t)
+        return remote(to_send.at[t], arrived.at[me], all_send.at[0], all_recv.at[0], t)
 
     def all_start(k, carry):
         all_copy(k).start()
@@ -384,12 +409,8 @@
     load_keys.wait()
     load_values.wait()
 
-    def all_wait(k, carry):
-        j = (me + k) % WIDE
-        remote(to_send.at[j], arrived.at[j], all_send.at[k], all_recv.at[j], j).wait_recv()
-        return carry
-
-    lax.fori_loop(1, WIDE, all_wait, 0)
+    received = arrived.at[pl.ds(0, WIDE - 1)]
+    remote(received, received, all_send.at[0], all_recv.at[0], c_peer).wait_recv()
 
     blocks = arrived[...].reshape(WIDE * 16, 256)
     query_rows = 2 * heads
@@ -457,54 +478,28 @@
 
     def piece_copy(owner, q, k, target):
         part = gathered.at[owner, pl.ds(pl.multiple_of(q * high, high), high)]
-        return remote(part, part, send2.at[q, k], recv2.at[q, owner], target)
+        arrives = near2.at[q] if k == 2 else recv2.at[q, owner]
+        return remote(part, part, send2.at[k], arrives, target)
 
     def piece_start(q, carry):
-        piece_copy(me, q, 3, y_peer).start()
-        piece_copy(me, q, 7, c_peer).start()
-
-        def body(p, inner):
-            piece_copy(me, q, p - 1, index(z_at(p), y, c)).start()
+        send_own(piece_copy, q)
+        return carry
+
+    lax.fori_loop(0, PIECES, piece_start, 0)
+
+    def pass_round(p, carry):
+        def body(q, inner):
+            pass_on(piece_copy, q, p)
+            pass_y(piece_copy, q, p - 1)
             return inner
 
-        return lax.fori_loop(1, 4, body, carry)
-
-    lax.fori_loop(0, PIECES, piece_start, 0)
-
-    def piece_arrival(owner, q):
-        piece_copy(owner, q, 0, c_peer).wait_recv()
-
-    def forward(q, p):
-        owner = index(z_at(p), y, c)
-        piece_arrival(owner, q)
-        piece_copy(owner, q, 3 + p, y_peer).start()
-        piece_copy(owner, q, 7 + p, c_peer).start()
-
-    def forward_y(q, p):
-        owner = index(z_at(p), 1 - y, c)
-        piece_arrival(owner, q)
-        piece_copy(owner, q, 11 + p, c_peer).start()
-
-    def stage_a(q):
-        def body(p, inner):
-            forward(q, p)
-            return inner
-
-        lax.fori_loop(1, 4, body, 0)
-
-    def stage_b(q):
-        def body(p, inner):
-            forward_y(q, p)
-            return inner
-
-        lax.fori_loop(0, 4, body, 0)
+        return lax.fori_loop(0, PIECES, body, carry)
+
+    lax.fori_loop(1, Z, pass_round, 0)
 
     def stage_c(q):
-        def body(j, inner):
-            piece_arrival(index(z_at(j // 2), (y + j) % Y, 1 - c), q)
-            return inner
-
-        lax.fori_loop(0, 8, body, 0)
+        part = gathered.at[pl.ds(0, WIDE // 2), pl.ds(0, high)]
+        remote(part, part, send2.at[2], near2.at[q], c_peer).wait_recv()
 
     total[...] = jnp.zeros_like(total)
     per_piece = groups // PIECES
@@ -519,13 +514,9 @@
         def _():
             q = g // per_piece
 
-            @pl.when(q < PIECES - 2)
-            def _():
-                stage_a(q + 2)
-
             @pl.when(q < PIECES - 1)
             def _():
-                stage_b(q + 1)
+                pass_y(piece_copy, q + 1, 3)
 
             stage_c(q)
 
@@ -543,36 +534,15 @@
 
         return carry
 
-    stage_a(0)
-    stage_a(1)
-    stage_b(0)
+    pass_y(piece_copy, 0, 3)
     lax.fori_loop(0, groups, multiply, 0)
     out[...] = total[...].astype(jnp.bfloat16)
 
-    def sent(k, carry):
-        stat_copy(k).wait_send()
-        all_copy(k).wait_send()
-        return carry
-
-    lax.fori_loop(1, WIDE, sent, 0)
-
-    def sent1(k, carry):
-        def body(h, inner):
-            own_copy(h, k, c_peer).wait_send()
-            return inner
-
-        return lax.fori_loop(0, HALVES, body, carry)
-
-    lax.fori_loop(0, 15, sent1, 0)
-
-    def sent2(k, carry):
-        def body(q, inner):
-            piece_copy(me, q, k, c_peer).wait_send()
-            return inner
-
-        return lax.fori_loop(0, PIECES, body, carry)
-
-    lax.fori_loop(0, 15, sent2, 0)
+    remote(others, others, stat_send.at[0], stat_recv.at[0], c_peer).wait_send()
+    left = to_send.at[pl.ds(0, WIDE - 1)]
+    remote(left, left, all_send.at[0], all_recv.at[0], c_peer).wait_send()
+    all_sent(shards, send1)
+    all_sent(gathered, send2)
 
 
 def fused(tokens, norm_gain, w_qkv, w_out, cache_k, cache_v, lengths):
@@ -605,14 +575,16 @@
             dma((WIDE,)),
             dma((heads // GROUP,)),
             dma((2,)),
-            dma((WIDE,)),
-            dma((WIDE,)),
-            dma((HALVES, 15)),
+            dma((1,)),
+            dma((1,)),
+            dma((3,)),
             dma((HALVES, WIDE)),
             dma((WIDE,)),
-            dma((WIDE,)),
-            dma((PIECES, 15)),
+            dma((1,)),
+            dma((1,)),
+            dma((3,)),
             dma((PIECES, WIDE)),
+            dma((PIECES,)),
             pltpu.VMEM((2, 8, 128), jnp.float32),
         ],
         compiler_params=pltpu.CompilerParams(

time: 67.5 us -> 62.5 us (0.926)
  Pallas kernels: 65.8 us -> 60.5 us
    pallas_call x1, Pallas kernels: 65.8 us -> 60.5 us  [fused(): pl.pallas_call(fused_kernel, out_shape=jax.ShapeDtypeStruct((rows, out_wi...]
where the time goes in v3:
time: 62.5 us; the launch traced here: 62.1 us
  Pallas kernels  60.5 us (97%)
  local copies, waits for them, and re-layouts  1.58 us (3%)
    pallas_call x1, Pallas kernels, fused(): pl.pallas_call(fused_kernel, out_shape=jax.ShapeDtypeStruct((rows, out_wi...  60.5 us
    unnamed x1, local copies, waits for them, and re-layouts  1.58 us

profile of v3, /device:TPU:0, one launch (start us, length us, event | category | flops | bytes accessed | tf_op | source)
XLA Modules:
  0.0 62.1 jit_solution(15276903662778420025)
XLA Ops:
  0.0 60.5 %shard_map.73 = bf16[64,1152]{1,0:T(8,128)(2,1)} custom-call(s32[2]{0:T(128)} %lengths.1, bf16[64,1152]{1,0:T(8,128)(2,1)} %bitcast.6, f32[16,1,1152]{2,1,0:T(1,128)} %bitcast.7, bf16[800,18432]{1,0:T(8,128)(2,1)} %bitcast.4, bf16[12288,1152]{1,0:T(8,128)(2,1)} %w_out.1, bf16[2,2048,256]{2,1,0:T(8,128)(2,1)} %cache_k.1, bf16[2,2048,256]{2,1,0:T(8,128)(2,1)} %cache_v.1), custom_call_target="tpu_custom_call" | custom-call | tf_op jit(solution)/shard_map/pallas_call | solution.py:557
  60.6 1.6 %copy.9 = bf16[2,32,1152]{2,1,0:T(8,128)(2,1)} copy(bf16[2,32,1152]{2,1,0:T(8,128)(2,1)} %bitcast.5) | data formatting | bytes 294912

commit v4 on v3

--- a/solution.py
+++ b/solution.py
@@ -327,13 +327,15 @@
     acc[...] = jnp.zeros_like(acc)
 
     others = stats.at[pl.ds(0, WIDE - 1)]
-    remote(others, others, stat_send.at[0], stat_recv.at[0], c_peer).wait_recv()
-    whole = jnp.sum(stats[...], axis=0)
-    features = float(depth * WIDE)
-    center = as_column(whole[0:1]) / features
-    spread = as_column(whole[1:2]) / features - center * center
-    columns[0] = jnp.broadcast_to(center, (rows, 128))
-    columns[1] = jnp.broadcast_to(lax.rsqrt(spread + norm_eps), (rows, 128))
+
+    def settle():
+        remote(others, others, stat_send.at[0], stat_recv.at[0], c_peer).wait_recv()
+        whole = jnp.sum(stats[...], axis=0)
+        features = float(depth * WIDE)
+        center = as_column(whole[0:1]) / features
+        spread = as_column(whole[1:2]) / features - center * center
+        columns[0] = jnp.broadcast_to(center, (rows, 128))
+        columns[1] = jnp.broadcast_to(lax.rsqrt(spread + norm_eps), (rows, 128))
 
     def project(owner):
         load_in(owner).wait()
@@ -361,6 +363,10 @@
             @pl.when(jnp.logical_and(p >= 1, p <= 4))
             def _():
                 pass_y(shard_copy, i, p - 1)
+
+            @pl.when(jnp.logical_and(p == 1, i == 0))
+            def _():
+                settle()
 
             late = 1 + i // 2
 

time: 62.5 us -> 62 us (level)
  no operation moved by 1% of the time
where the time goes in v4:
time: 62 us; the launch traced here: 61.7 us
  Pallas kernels  60.1 us (97%)
  local copies, waits for them, and re-layouts  1.58 us (3%)
    pallas_call x1, Pallas kernels, fused(): pl.pallas_call(fused_kernel, out_shape=jax.ShapeDtypeStruct((rows, out_wi...  60.1 us
    unnamed x1, local copies, waits for them, and re-layouts  1.58 us

profile of v4, /device:TPU:0, one launch (start us, length us, event | category | flops | bytes accessed | tf_op | source)
XLA Modules:
  0.0 61.7 jit_solution(2709740637274014462)
XLA Ops:
  0.0 60.1 %shard_map.73 = bf16[64,1152]{1,0:T(8,128)(2,1)} custom-call(s32[2]{0:T(128)} %lengths.1, bf16[64,1152]{1,0:T(8,128)(2,1)} %bitcast.6, f32[16,1,1152]{2,1,0:T(1,128)} %bitcast.7, bf16[800,18432]{1,0:T(8,128)(2,1)} %bitcast.4, bf16[12288,1152]{1,0:T(8,128)(2,1)} %w_out.1, bf16[2,2048,256]{2,1,0:T(8,128)(2,1)} %cache_k.1, bf16[2,2048,256]{2,1,0:T(8,128)(2,1)} %cache_v.1), custom_call_target="tpu_custom_call" | custom-call | tf_op jit(solution)/shard_map/pallas_call | solution.py:563
  60.1 1.6 %copy.9 = bf16[2,32,1152]{2,1,0:T(8,128)(2,1)} copy(bf16[2,32,1152]{2,1,0:T(8,128)(2,1)} %bitcast.5) | data formatting | bytes 294912
